TPU v7x, 32 devices: a whole 2x2x4 slice. The times are simulated.
32 devices in a mesh: sample: 8 (over y, x, core), protein: 4 (over z).
Axes of the slice: x: 2, y: 2, z: 4, core: 2. Of those that a mesh axis runs over, the one named last changes fastest.
Arguments:
- proteins: bfloat16 [4096, 2048], P('sample'), may hold values from -34 to 34
- dosage: bfloat16 [4096, 512], P('sample'), may hold values from 0 to 2, as said below
Outputs:
- scores: float32 [512, 2048], P('sample', 'protein')
Inputs may be any that keep to these rules, and one draw needn't show every extreme that they name: `dosage`: allele dosages, whole numbers.
All inputs are finite; a program needn't handle non-finite values.
Results may differ from a plain program's by a relative error of at most 0.0003.
Values sent between devices are 32-bit elements; how exact they have to be, the bound alone decides.
A program may use at most 128 MiB of HBM per device.

v0:
```python
import math

import jax
import jax.numpy as jnp
from jax import lax
from jax.sharding import PartitionSpec as P


def broadcast(value, axis, root):
    mine = lax.axis_index(axis) == root
    return lax.psum(jnp.where(mine, value, jnp.zeros_like(value)), axis)


def right_solve(factor, rows):
    return jax.scipy.linalg.solve_triangular(factor, rows.T, lower=True).T


def split_cholesky(matrix):
    order = matrix.shape[0]
    if order <= 128 or order % 2 != 0:
        return jnp.linalg.cholesky(matrix)
    half = order // 2
    leading = split_cholesky(matrix[:half, :half])
    below = right_solve(leading, matrix[half:, :half])
    trailing = matrix[half:, half:] - jnp.dot(below, below.T, precision=lax.Precision.HIGHEST)
    trailing_factor = split_cholesky(trailing)
    upper_rows = jnp.concatenate([leading, jnp.zeros((half, order - half), jnp.float32)], 1)
    lower_rows = jnp.concatenate([below, trailing_factor], 1)
    return jnp.concatenate([upper_rows, lower_rows], 0)


def body(proteins, dosage):
    total_proteins = proteins.shape[1]
    groups = lax.axis_size("protein")
    block_width = total_proteins // groups
    column = lax.axis_index("protein")
    sample_count = proteins.shape[0] * lax.axis_size("sample")
    variant_rows = dosage.shape[1] // lax.axis_size("sample")
    contract = (((0,), (0,)), ((), ()))
    own_proteins = lax.dynamic_slice_in_dim(proteins, column * block_width, block_width, 1)
    gram_part = lax.dot_general(
        proteins, own_proteins, contract, preferred_element_type=jnp.float32
    )
    cross_part = lax.dot_general(dosage, own_proteins, contract, preferred_element_type=jnp.float32)
    protein_sums = jnp.sum(own_proteins, axis=0, dtype=jnp.float32)
    dose_sums = jnp.sum(dosage, axis=0, dtype=jnp.float32)
    dose_squares = jnp.sum(dosage * dosage, axis=0, dtype=jnp.float32)
    gram_total, protein_sums, dose_sums, dose_squares = lax.psum(
        (gram_part, protein_sums, dose_sums, dose_squares), "sample"
    )
    cross = lax.psum_scatter(cross_part, "sample", scatter_dimension=0, tiled=True)
    row_start = lax.axis_index("sample") * variant_rows
    dose_sums = lax.dynamic_slice_in_dim(dose_sums, row_start, variant_rows, 0)
    dose_squares = lax.dynamic_slice_in_dim(dose_squares, row_start, variant_rows, 0)
    gram = gram_total / sample_count
    means = dose_sums / sample_count
    spread = jnp.sqrt(dose_squares / sample_count - means * means + 1e-05)
    centred = (cross - means[:, None] * protein_sums[None, :]) / (
        spread[:, None] * math.sqrt(sample_count)
    )
    working = gram
    diagonal_block = jnp.zeros((block_width, block_width), jnp.float32)
    row_blocks = []
    for section in range(groups):
        current = working[section * block_width : (section + 1) * block_width]
        section_factor = split_cholesky(current)
        diagonal_block = jnp.where(column == section, section_factor, diagonal_block)
        if section < groups - 1:
            lower_rows = working[(section + 1) * block_width :]
            panel_own = right_solve(section_factor, lower_rows)
            panel = broadcast(panel_own, "protein", section)
            relative = jnp.clip(column - section - 1, 0, groups - section - 2)
            my_block = lax.dynamic_slice_in_dim(panel, relative * block_width, block_width, 0)
            my_block = jnp.where(column > section, my_block, jnp.zeros_like(my_block))
            row_blocks.append(my_block)
            update = jnp.dot(panel, my_block.T, precision=lax.Precision.HIGHEST)
            working = working.at[(section + 1) * block_width :].add(-update)
    remaining = centred
    for section in range(groups - 1):
        finished = right_solve(diagonal_block, remaining)
        solved_block = broadcast(finished, "protein", section)
        remaining = remaining - jnp.dot(
            solved_block, row_blocks[section].T, precision=lax.Precision.HIGHEST
        )
    scores = right_solve(diagonal_block, remaining)
    return scores


def solution(mesh):
    in_specs = (P("sample", None), P("sample", None))
    out_specs = P("sample", "protein")
    return jax.shard_map(body, mesh=mesh, in_specs=in_specs, out_specs=out_specs, check_vma=False)
```

profile of v0, /device:TPU:25, one launch (start us, length us, event | category | flops | bytes accessed | tf_op | source)
XLA Modules:
  0.0 1197.1 jit_solution(13253200569964285507)
XLA Ops:
  6.5 5.0 convolution_bitcast_fusion
  11.7 82.0 %all-reduce.21.cloned.1.call-done = f32[2048,512]{0,1:T(8,128)} async-done(((f32[2048,512]{0,1:T(8,128)}), f32[2048,512]{0,1:T(8,128)}) %all-reduce.21.cloned.1.call-update) | async-done | bytes 4194320 | tf_op jit(solution)/shard_map/psum | solution.py:48
  99.1 11.7 cholesky.254
  112.2 9.8 custom-call.39
  125.5 11.7 cholesky.265
  138.8 4.6 while.25
  143.5 19.7 %custom-call.40 = f32[2,128,128]{1,2,0:T(8,128)S(1)} custom-call(f32[2,128,128]{2,1,0:T(8,128)S(1)} %get-tuple-element.121), custom_call_target="InvertDiagBlocksLowerTriangular" | custom-call | tf_op jit(solution)/shard_map/jit(_solve_triangular)/triangular_solve | solution.py:15
  165.9 11.7 cholesky.276
  178.8 9.8 custom-call.41
  193.2 11.7 cholesky.287
  206.3 7.5 while.22
  213.9 39.5 %custom-call.23 = f32[4,128,128]{1,2,0:T(8,128)S(1)} custom-call(f32[4,128,128]{2,1,0:T(8,128)S(1)} %get-tuple-element.68), custom_call_target="InvertDiagBlocksLowerTriangular" | custom-call | tf_op jit(solution)/shard_map/jit(_solve_triangular)/triangular_solve | solution.py:15
  269.1 119.3 %all-reduce.23.cloned.1.call-done = f32[1536,512]{1,0:T(8,128)} async-done(((f32[1536,512]{1,0:T(8,128)}), f32[1536,512]{1,0:T(8,128)}) %all-reduce.23.cloned.1.call-update) | async-done | bytes 3145744 | tf_op jit(solution)/shard_map/psum | solution.py:11
  388.4 8.2 fusion
  396.7 11.7 cholesky.298
  409.8 9.8 custom-call.42
  421.2 11.7 cholesky.309
  438.8 20.4 %custom-call.43 = f32[2,128,128]{1,2,0:T(8,128)} custom-call(f32[2,128,128]{2,1,0:T(8,128)S(1)} %get-tuple-element.122), custom_call_target="InvertDiagBlocksLowerTriangular" | custom-call | tf_op jit(solution)/shard_map/jit(_solve_triangular)/triangular_solve | solution.py:15
  468.5 11.7 cholesky.320
  482.2 11.3 custom-call.44
  501.7 13.2 %cholesky.331 = f32[128,128]{1,0:T(8,128)} custom-call(f32[128,128]{1,0:T(8,128)} %fusion.188), custom_call_target="Cholesky" | custom-call | tf_op jit(solution)/shard_map/jit(cholesky)/cholesky | solution.py:21
  519.2 11.6 while.23
  531.5 40.3 %custom-call.24 = f32[4,128,128]{1,2,0:T(8,128)S(1)} custom-call(f32[4,128,128]{2,1,0:T(8,128)} %copy-done.31), custom_call_target="InvertDiagBlocksLowerTriangular" | custom-call | tf_op jit(solution)/shard_map/jit(_solve_triangular)/triangular_solve | solution.py:15
  599.2 80.1 %all-reduce.25.cloned.1.call-done = f32[1024,512]{1,0:T(8,128)} async-done(((f32[1024,512]{1,0:T(8,128)}), f32[1024,512]{1,0:T(8,128)}) %all-reduce.25.cloned.1.call-update) | async-done | bytes 2097168 | tf_op jit(solution)/shard_map/psum | solution.py:11
  679.4 5.5 negate_add_fusion
  687.2 11.7 cholesky.342
  700.1 9.8 custom-call.45
  713.5 11.9 cholesky.353
  731.2 19.7 %custom-call.46 = f32[2,128,128]{1,2,0:T(8,128)S(1)} custom-call(f32[2,128,128]{2,1,0:T(8,128)S(1)} %get-tuple-element.123), custom_call_target="InvertDiagBlocksLowerTriangular" | custom-call | tf_op jit(solution)/shard_map/jit(_solve_triangular)/triangular_solve | solution.py:15
  752.5 11.7 cholesky.364
  765.6 9.8 custom-call.47
  780.5 13.2 %cholesky.375 = f32[128,128]{1,0:T(8,128)} custom-call(f32[128,128]{1,0:T(8,128)} %fusion.182), custom_call_target="Cholesky" | custom-call | tf_op jit(solution)/shard_map/jit(cholesky)/cholesky | solution.py:21
  798.0 11.3 while.24
  809.3 40.3 %custom-call.25 = f32[4,128,128]{1,2,0:T(8,128)} custom-call(f32[4,128,128]{2,1,0:T(8,128)S(1)} %get-tuple-element.84), custom_call_target="InvertDiagBlocksLowerTriangular" | custom-call | tf_op jit(solution)/shard_map/jit(_solve_triangular)/triangular_solve | solution.py:15
  868.8 12.2 %all-reduce.12 = (f32[512]{0:T(512)S(1)}, f32[512]{0:T(512)S(1)}, f32[512]{0:T(512)S(1)}) all-reduce(f32[512]{0:T(512)S(1)} %get-tuple-element.130, f32[512]{0:T(512)S(1)} %get-tuple-element.129, f32[512]{0:T(512)S(1)} %convert_reduce_fusion.1), channel_id=1, replica_groups=mesh['sample'=8,'protein'=4] {'sample'}, use_global_device_ids=true, to_apply=%region_12.16 | all-reduce | flops 1536 | bytes 12288 | tf_op jit(solution)/shard_map/psum | solution.py:48
  882.8 36.4 %all-reduce.27.cloned.1.call-done = f32[512,512]{1,0:T(8,128)} async-done(((f32[512,512]{1,0:T(8,128)}), f32[512,512]{1,0:T(8,128)}) %all-reduce.27.cloned.1.call-update) | async-done | bytes 1048592 | tf_op jit(solution)/shard_map/psum | solution.py:11
  922.7 11.7 cholesky.386
  935.8 9.8 custom-call.48
  946.4 11.8 cholesky.397
  964.3 19.7 %custom-call.49 = f32[2,128,128]{1,2,0:T(8,128)S(1)} custom-call(f32[2,128,128]{2,1,0:T(8,128)S(1)} %get-tuple-element.124), custom_call_target="InvertDiagBlocksLowerTriangular" | custom-call | tf_op jit(solution)/shard_map/jit(_solve_triangular)/triangular_solve | solution.py:15
  986.4 11.7 cholesky.408
  999.3 9.8 custom-call.50
  1010.0 11.7 cholesky.419
  1025.9 7.5 while.29
  1033.4 39.3 %custom-call.54 = f32[4,128,128]{1,2,0:T(8,128)S(1)} custom-call(f32[4,128,128]{2,1,0:T(8,128)S(1)} %get-tuple-element.128), custom_call_target="InvertDiagBlocksLowerTriangular" | custom-call | tf_op jit(solution)/shard_map/jit(_solve_triangular)/triangular_solve | solution.py:15
  1075.1 32.5 %all-reduce.29.cloned.1.call-done = f32[64,512]{1,0:T(8,128)} async-done(((f32[64,512]{1,0:T(8,128)}), f32[64,512]{1,0:T(8,128)}) %all-reduce.29.cloned.1.call-update) | async-done | bytes 131088 | tf_op jit(solution)/shard_map/psum | solution.py:11
  1112.4 34.2 %all-reduce.31.cloned.1.call-done = f32[64,512]{1,0:T(8,128)} async-done(((f32[64,512]{1,0:T(8,128)}), f32[64,512]{1,0:T(8,128)}) %all-reduce.31.cloned.1.call-update) | async-done | bytes 131088 | tf_op jit(solution)/shard_map/psum | solution.py:11
  1151.4 34.3 %all-reduce.33.cloned.1.call-done = f32[64,512]{1,0:T(8,128)} async-done(((f32[64,512]{1,0:T(8,128)}), f32[64,512]{1,0:T(8,128)}) %all-reduce.33.cloned.1.call-update) | async-done | bytes 131088 | tf_op jit(solution)/shard_map/psum | solution.py:11
  (399 shorter events, 232.9 us)
Async XLA Ops:
  6.5 87.1 %all-reduce.21.cloned.1.call-start = ((), (), s32[]{:S(2)}) async-start(), calls=%async_computation.1 | async-start | bytes 8388608 | tf_op jit(solution)/shard_map/psum | solution.py:48
  11.6 376.8 %all-reduce.23.cloned.1.call-start = ((), (), s32[]{:S(2)}) async-start(), calls=%async_computation.2 | async-start | bytes 6291456 | tf_op jit(solution)/shard_map/psum | solution.py:11
  96.2 1.9 copy-start
  138.7 67.4 %copy-start.15 = (f32[256,256]{1,0:T(8,128)}, f32[256,256]{1,0:T(8,128)S(1)}, u32[]{:S(2)}) copy-start(f32[256,256]{1,0:T(8,128)S(1)} %get-tuple-element.236) | copy-start | bytes 786436
  164.3 41.9 %copy-start.9 = (f32[256,256]{1,0:T(8,128)}, f32[256,256]{1,0:T(8,128)S(1)}, u32[]{:S(2)}) copy-start(f32[256,256]{1,0:T(8,128)S(1)} %fusion.90) | copy-start | bytes 786436
  178.8 27.4 %copy-start.20 = (f32[128,128]{1,0:T(8,128)}, f32[128,128]{1,0:T(8,128)S(1)}, u32[]{:S(2)}) copy-start(f32[128,128]{1,0:T(8,128)S(1)} %get-tuple-element.211) | copy-start | bytes 196612
  189.3 16.9 %copy-start.23 = (f32[128,128]{0,1:T(8,128)}, f32[128,128]{0,1:T(8,128)S(1)}, u32[]{:S(2)}) copy-start(f32[128,128]{0,1:T(8,128)S(1)} %copy.75) | copy-start | bytes 196612
  206.1 7.7 copy-start.24
  253.4 5.0 copy-start.30
  255.4 2.9 copy-start.2
  269.1 410.3 %all-reduce.25.cloned.1.call-start = ((), (), s32[]{:S(2)}) async-start(), calls=%async_computation.3 | async-start | bytes 4194304 | tf_op jit(solution)/shard_map/psum | solution.py:11
  465.4 51.7 %copy-start.11 = (f32[256,256]{1,0:T(8,128)}, f32[256,256]{1,0:T(8,128)S(1)}, u32[]{:S(2)}) copy-start(f32[256,256]{1,0:T(8,128)S(1)} %fusion.89) | copy-start | bytes 786436
  466.9 0.7 copy-start.19
  497.1 20.0 %copy-start.25 = (f32[128,128]{0,1:T(8,128)S(1)}, f32[128,128]{0,1:T(8,128)}, u32[]{:S(2)}) copy-start(f32[128,128]{0,1:T(8,128)} %copy.91) | copy-start | bytes 196612
  517.1 2.1 copy-start.26
  530.8 0.7 copy-start.31
  571.8 4.3 copy-start.6
  573.7 4.9 copy-start.1
  576.2 2.4 copy-start.7
  578.6 0.8 copy-start.8
  593.4 287.8 %reduce-scatter.4.cloned.1.call-start = ((), (), s32[]{:S(2)}) async-start(), calls=%async_computation.8 | async-start | bytes 1179648 | tf_op jit(solution)/shard_map/reduce_scatter | solution.py:51
  598.7 320.4 %all-reduce.27.cloned.1.call-start = ((), (), s32[]{:S(2)}) async-start(), calls=%async_computation.4 | async-start | bytes 2097152 | tf_op jit(solution)/shard_map/psum | solution.py:11
  684.9 1.3 copy-start.3
  712.2 39.8 %copy-start.4 = (f32[1024,512]{0,1:T(8,128)S(1)}, f32[1024,512]{0,1:T(8,128)}, u32[]{:S(2)}) copy-start(f32[1024,512]{0,1:T(8,128)} %copy-done.3) | copy-start | bytes 6291460
  731.1 46.3 %copy-start.32 = (s32[2,2]{1,0:T(2,128)}, s32[2,2]{1,0:T(2,128)S(1)}, u32[]{:S(2)}) copy-start(s32[2,2]{1,0:T(2,128)S(1)} %get-tuple-element.637) | copy-start | bytes 52
  752.0 43.9 %copy-start.13 = (f32[256,256]{1,0:T(8,128)}, f32[256,256]{1,0:T(8,128)S(1)}, u32[]{:S(2)}) copy-start(f32[256,256]{1,0:T(8,128)S(1)} %fusion.88) | copy-start | bytes 786436
  765.6 32.4 %copy-start.22 = (f32[128,128]{1,0:T(8,128)}, f32[128,128]{1,0:T(8,128)S(1)}, u32[]{:S(2)}) copy-start(f32[128,128]{1,0:T(8,128)S(1)} %get-tuple-element.203) | copy-start | bytes 196612
  795.9 2.2 copy-start.27
  863.8 4.9 copy-start.18
  867.4 240.1 %all-reduce.29.cloned.1.call-start = ((), (), s32[]{:S(2)}) async-start(), calls=%async_computation.5 | async-start | bytes 262144 | tf_op jit(solution)/shard_map/psum | solution.py:11
  922.6 37.8 %copy-start.33 = (s32[2,2]{1,0:T(2,128)S(1)}, s32[2,2]{1,0:T(2,128)}, u32[]{:S(2)}) copy-start(s32[2,2]{1,0:T(2,128)} %copy-done.32) | copy-start | bytes 52
  964.3 58.7 %copy-start.10 = (f32[256,256]{1,0:T(8,128)S(1)}, f32[256,256]{1,0:T(8,128)}, u32[]{:S(2)}) copy-start(f32[256,256]{1,0:T(8,128)} %copy-done.9) | copy-start | bytes 786436
  964.3 58.7 %copy-start.12 = (f32[256,256]{1,0:T(8,128)S(1)}, f32[256,256]{1,0:T(8,128)}, u32[]{:S(2)}) copy-start(f32[256,256]{1,0:T(8,128)} %copy-done.11) | copy-start | bytes 786436
  964.3 58.7 %copy-start.14 = (f32[256,256]{1,0:T(8,128)S(1)}, f32[256,256]{1,0:T(8,128)}, u32[]{:S(2)}) copy-start(f32[256,256]{1,0:T(8,128)} %copy-done.13) | copy-start | bytes 786436
  964.3 58.7 %copy-start.16 = (f32[256,256]{1,0:T(8,128)S(1)}, f32[256,256]{1,0:T(8,128)}, u32[]{:S(2)}) copy-start(f32[256,256]{1,0:T(8,128)} %copy-done.15) | copy-start | bytes 786436
  964.3 58.7 %copy-start.17 = (f32[256,256]{1,0:T(8,128)S(1)}, f32[256,256]{1,0:T(8,128)}, u32[]{:S(2)}) copy-start(f32[256,256]{1,0:T(8,128)} %get-tuple-element.234) | copy-start | bytes 786436
  964.3 58.7 %copy-start.21 = (f32[128,128]{1,0:T(8,128)S(1)}, f32[128,128]{1,0:T(8,128)}, u32[]{:S(2)}) copy-start(f32[128,128]{1,0:T(8,128)} %copy-done.20) | copy-start | bytes 196612
  1023.0 49.7 %copy-start.28 = (f32[512,64]{0,1:T(8,128)S(1)}, f32[512,64]{0,1:T(8,128)}, u32[]{:S(2)}) copy-start(f32[512,64]{0,1:T(8,128)} %fusion.302) | copy-start | bytes 393220
  1025.8 81.8 %copy-start.29 = (f32[64,512]{1,0:T(8,128)S(1)}, f32[64,512]{1,0:T(8,128)}, u32[]{:S(2)}) copy-start(f32[64,512]{1,0:T(8,128)} %reduce-scatter.4.cloned.1.call-done) | copy-start | bytes 393220
  1075.1 71.5 %all-reduce.31.cloned.1.call-start = ((), (), s32[]{:S(2)}) async-start(), calls=%async_computation.6 | async-start | bytes 262144 | tf_op jit(solution)/shard_map/psum | solution.py:11
  1110.2 75.5 %copy-start.5 = (f32[512,512]{1,0:T(8,128)S(1)}, f32[512,512]{1,0:T(8,128)}, u32[]{:S(2)}) copy-start(f32[512,512]{1,0:T(8,128)} %all-reduce.27.cloned.1.call-done) | copy-start | bytes 3145732
  1112.4 73.3 %all-reduce.33.cloned.1.call-start = ((), (), s32[]{:S(2)}) async-start(), calls=%async_computation.7 | async-start | bytes 262144 | tf_op jit(solution)/shard_map/psum | solution.py:11
Sparse Core Ops, SparseCore 0:
  11.7 81.9 all-reduce.20
  269.2 119.1 all-reduce.22
  593.5 85.8 all-reduce.24
  682.4 36.8 reduce-scatter.3
  867.6 51.5 all-reduce.26
  1075.2 32.3 all-reduce.28
  1112.5 34.0 all-reduce.30
  1151.5 34.1 all-reduce.32
where the time goes:
time: 1210 us; the launch traced here: 1200 us
  other arithmetic  565 us (47%)
  waiting for transfers between devices  419 us (35%)
  matrix products  95.5 us (8%)
  local copies, waits for them, and re-layouts  88.3 us (7%)
  between operations  15.6 us (1%)
  blocking collectives  12.2 us (1%)
    psum x6, waiting for transfers between devices, broadcast(): return lax.psum(jnp.where(mine, value, jnp.zeros_like(value)), axis)  337 us
    another operation x30, other arithmetic, right_solve(): return jax.scipy.linalg.solve_triangular(factor, rows.T, lower=True).T  332 us
    another operation x48, other arithmetic, split_cholesky(): return jnp.linalg.cholesky(matrix)  203 us
    psum x1, waiting for transfers between devices, body(): lax.psum((gram_part, protein_sums, dose_sums, dose_squares), 'sample')  82 us
    another operation x69, matrix products, right_solve(): return jax.scipy.linalg.solve_triangular(factor, rows.T, lower=True).T  54 us
    another operation x63, local copies, waits for them, and re-layouts, right_solve(): return jax.scipy.linalg.solve_triangular(factor, rows.T, lower=True).T  37.3 us
    another operation x36, local copies, waits for them, and re-layouts  30.1 us
  transfers between devices with their start and end apart: 8, of which 7 were waited for; matrix products, arithmetic and copies ran while one was open for 16% of the time, Pallas kernels for 0%

commit v1 on v0

v1 whole, which is shorter than its diff:
```python
import math

import jax
import jax.numpy as jnp
from jax import lax
from jax.experimental import pallas as pl
from jax.experimental.pallas import tpu as pltpu
from jax.sharding import PartitionSpec as P

SUB = 8
HALF = 128
WIDE = 256
CHUNK = 512


def split(value):
    high = value.astype(jnp.bfloat16)
    low = (value - high.astype(jnp.float32)).astype(jnp.bfloat16)
    return high, low


def dot_nt(left, right):
    return lax.dot_general(
        left, right, (((1,), (1,)), ((), ())), preferred_element_type=jnp.float32
    )


def product_nt(left, right):
    left_high, left_low = left
    right_high, right_low = right
    return (
        dot_nt(left_high, right_high)
        + dot_nt(left_low, right_high)
        + dot_nt(left_high, right_low)
    )


def exact_dot(left, right):
    return jnp.dot(
        left, right, precision=lax.Precision.HIGHEST, preferred_element_type=jnp.float32
    )


def exact_nt(left, right):
    return lax.dot_general(
        left,
        right,
        (((1,), (1,)), ((), ())),
        precision=lax.Precision.HIGHEST,
        preferred_element_type=jnp.float32,
    )


def inverse_factor(work, inverse):
    for start in range(0, HALF, SUB):
        stop = start + SUB
        rows = work[start:stop, :]
        row = [jnp.broadcast_to(rows[k : k + 1, :], (SUB, 2 * HALF)) for k in range(SUB)]
        col = [
            jnp.broadcast_to(rows[:, start + k : start + k + 1], (SUB, HALF)) for k in range(SUB)
        ]
        entry = [
            [jnp.broadcast_to(col[k][i : i + 1, :], (SUB, HALF)) for k in range(i + 1)]
            for i in range(SUB)
        ]
        scale = [None] * SUB
        lower = [[None] * SUB for _ in range(SUB)]
        for k in range(SUB):
            scale[k] = lax.rsqrt(entry[k][k])
            for i in range(k + 1, SUB):
                lower[i][k] = entry[i][k] * scale[k]
            for i in range(k + 1, SUB):
                for m in range(k + 1, i + 1):
                    entry[i][m] = entry[i][m] - lower[i][k] * lower[m][k]
        solved = [None] * SUB
        wide = lambda value: jnp.concatenate([value, value], 1)
        for i in range(SUB):
            total = row[i]
            for k in range(i):
                total = total - wide(lower[i][k]) * solved[k]
            solved[i] = total * wide(scale[i])
        for i in range(SUB):
            inverse[start + i : start + i + 1, :] = solved[i][0:1, HALF:]
        if stop == HALF:
            break
        twice = [None] * SUB
        for i in reversed(range(SUB)):
            total = solved[i]
            for k in range(i + 1, SUB):
                total = total - wide(lower[k][i]) * twice[k]
            twice[i] = total * wide(scale[i])
        for top in range(stop, HALF, SUB):
            block = work[top : top + SUB, :]
            for k in range(SUB):
                factor = jnp.broadcast_to(
                    work[top : top + SUB, start + k : start + k + 1], (SUB, HALF)
                )
                block = block - wide(factor) * twice[k]
            work[top : top + SUB, :] = block


def factor_kernel(gram, centred, out, matrix, work, first, second, full, high, low, sem):
    panels, proteins, _ = gram.shape
    variants = centred.shape[0]
    total = proteins + variants
    copies = [
        pltpu.make_async_copy(gram.at[p], matrix.at[p, pl.ds(0, proteins), :], sem.at[p])
        for p in range(panels)
    ]
    for copy in copies:
        copy.start()
    for p in range(panels):
        matrix[p, proteins:, :] = centred[:, p * WIDE : (p + 1) * WIDE]
    for copy in copies:
        copy.wait()
    eye = (
        lax.broadcasted_iota(jnp.int32, (HALF, HALF), 0)
        == lax.broadcasted_iota(jnp.int32, (HALF, HALF), 1)
    ).astype(jnp.float32)

    def step(k, carry):
        top = pl.multiple_of(k * WIDE, WIDE)
        mid = pl.multiple_of(k * WIDE + HALF, HALF)
        work[:, :HALF] = matrix[k, pl.ds(top, HALF), :HALF]
        work[:, HALF:] = eye
        inverse_factor(work, first)
        below = exact_nt(matrix[k, pl.ds(mid, HALF), :HALF], first[...])
        work[:, :HALF] = matrix[k, pl.ds(mid, HALF), HALF:] - exact_nt(below, below)
        work[:, HALF:] = eye
        inverse_factor(work, second)
        full[:HALF, :HALF] = first[...]
        full[:HALF, HALF:] = jnp.zeros((HALF, HALF), jnp.float32)
        full[HALF:, :HALF] = -exact_dot(second[...], exact_dot(below, first[...]))
        full[HALF:, HALF:] = second[...]
        inverse = split(full[...])

        def panel_chunk(i, carry):
            base = pl.multiple_of(total - CHUNK * (i + 1), 64)
            block = product_nt(split(matrix[k, pl.ds(base, CHUNK), :]), inverse)
            block_high, block_low = split(block)
            high[pl.ds(base, CHUNK), :] = block_high
            low[pl.ds(base, CHUNK), :] = block_low

            @pl.when(i == 0)
            def _():
                out[k] = block[CHUNK - variants :, :]

            return carry

        rest = total - WIDE * (k + 1)
        lax.fori_loop(0, (rest + CHUNK - 1) // CHUNK, panel_chunk, 0)

        def update(m, carry):
            at = pl.multiple_of(m * WIDE, WIDE)
            right = (high[pl.ds(at, WIDE), :], low[pl.ds(at, WIDE), :])

            def update_chunk(i, carry):
                base = pl.multiple_of(total - CHUNK * (i + 1), 64)
                rows = pl.ds(base, CHUNK)
                matrix[m, rows, :] = matrix[m, rows, :] - product_nt(
                    (high[rows, :], low[rows, :]), right
                )
                return carry

            return lax.fori_loop(0, (total - m * WIDE + CHUNK - 1) // CHUNK, update_chunk, carry)

        lax.fori_loop(k + 1, panels, update, 0)
        return carry

    lax.fori_loop(0, panels, step, 0)


def whitened(gram, centred):
    panels, proteins, _ = gram.shape
    variants = centred.shape[0]
    total = proteins + variants
    return pl.pallas_call(
        factor_kernel,
        out_shape=jax.ShapeDtypeStruct((panels, variants, WIDE), jnp.float32),
        in_specs=[
            pl.BlockSpec(memory_space=pl.ANY),
            pl.BlockSpec(memory_space=pltpu.VMEM),
        ],
        out_specs=pl.BlockSpec(memory_space=pltpu.VMEM),
        scratch_shapes=[
            pltpu.VMEM((panels, total, WIDE), jnp.float32),
            pltpu.VMEM((HALF, 2 * HALF), jnp.float32),
            pltpu.VMEM((HALF, HALF), jnp.float32),
            pltpu.VMEM((HALF, HALF), jnp.float32),
            pltpu.VMEM((WIDE, WIDE), jnp.float32),
            pltpu.VMEM((total, WIDE), jnp.bfloat16),
            pltpu.VMEM((total, WIDE), jnp.bfloat16),
            pltpu.SemaphoreType.DMA((panels,)),
        ],
        compiler_params=pltpu.CompilerParams(vmem_limit_bytes=48 * 1024 * 1024),
    )(gram, centred)


def body(proteins, dosage):
    total_proteins = proteins.shape[1]
    groups = lax.axis_size("protein")
    block_width = total_proteins // groups
    column = lax.axis_index("protein")
    sample_count = proteins.shape[0] * lax.axis_size("sample")
    variant_rows = dosage.shape[1] // lax.axis_size("sample")
    contract = (((0,), (0,)), ((), ()))
    own_proteins = lax.dynamic_slice_in_dim(proteins, column * block_width, block_width, 1)
    gram_part = jnp.stack(
        [
            lax.dot_general(
                proteins,
                own_proteins[:, p * WIDE : (p + 1) * WIDE],
                contract,
                preferred_element_type=jnp.float32,
            )
            for p in range(block_width // WIDE)
        ]
    )
    cross_part = lax.dot_general(dosage, own_proteins, contract, preferred_element_type=jnp.float32)
    protein_sums = jnp.sum(own_proteins, axis=0, dtype=jnp.float32)
    dose_sums = jnp.sum(dosage, axis=0, dtype=jnp.float32)
    dose_squares = jnp.sum(dosage * dosage, axis=0, dtype=jnp.float32)
    gram_total, protein_sums, dose_sums, dose_squares = lax.psum(
        (gram_part, protein_sums, dose_sums, dose_squares), "sample"
    )
    cross = lax.psum_scatter(cross_part, "sample", scatter_dimension=0, tiled=True)
    row_start = lax.axis_index("sample") * variant_rows
    dose_sums = lax.dynamic_slice_in_dim(dose_sums, row_start, variant_rows, 0)
    dose_squares = lax.dynamic_slice_in_dim(dose_squares, row_start, variant_rows, 0)
    gram = gram_total / sample_count
    means = dose_sums / sample_count
    spread = jnp.sqrt(dose_squares / sample_count - means * means + 1e-05)
    centred = (cross - means[:, None] * protein_sums[None, :]) / (
        spread[:, None] * math.sqrt(sample_count)
    )
    gram = lax.all_gather(gram, "protein", axis=0, tiled=True)
    centred = lax.all_gather(centred, "protein", axis=1, tiled=True)
    scores = whitened(gram, centred)
    own = block_width // WIDE
    scores = lax.dynamic_slice_in_dim(scores, column * own, own, 0)
    return jnp.concatenate([scores[p] for p in range(own)], 1)


def solution(mesh):
    in_specs = (P("sample", None), P("sample", None))
    out_specs = P("sample", "protein")
    return jax.shard_map(body, mesh=mesh, in_specs=in_specs, out_specs=out_specs, check_vma=False)
```

time: 1210 us -> 567 us (0.47)
  other arithmetic: 565 us -> 9.03 us
  Pallas kernels: 0 us -> 136 us
  matrix products: 95.5 us -> 4.76 us
  local copies, waits for them, and re-layouts: 88.3 us -> 6.38 us
  waiting for transfers between devices: 419 us -> 370 us
  blocking collectives: 12.2 us -> 24.4 us
    another operation x78 -> x1, other arithmetic: 535 us -> 2.24 us  [body(): jnp.stack([lax.dot_general(proteins, own_proteins[:, p * WIDE:(p + 1) * W...]
    psum x6 -> x0, waiting for transfers between devices: 337 us -> none  [broadcast(): return lax.psum(jnp.where(mine, value, jnp.zeros_like(value)), axis)]
    all_gather x0 -> x1, waiting for transfers between devices: none -> 274 us  [body(): gram = lax.all_gather(gram, 'protein', axis=0, tiled=True)]
    pallas_call x0 -> x1, Pallas kernels: none -> 136 us  [whitened(): pl.pallas_call(factor_kernel, out_shape=jax.ShapeDtypeStruct((panels, var...]
    another operation x99 -> x0, local copies, waits for them, and re-layouts: 67.4 us -> none  [the longest x63 37.3 us: right_solve(): return jax.scipy.linalg.solve_triangular(factor, rows.T, lower=True).T]
    another operation x69 -> x0, matrix products: 54 us -> none  [right_solve(): return jax.scipy.linalg.solve_triangular(factor, rows.T, lower=True).T]
    dot_general x19 -> x2, matrix products: 38.7 us -> 3.3 us  [body(): lax.dot_general(proteins, own_proteins[:, p * WIDE:(p + 1) * WIDE], contr...]
    reduce_scatter x1, waiting for transfers between devices: 0.01 us -> 17 us  [body(): lax.psum_scatter(cross_part, 'sample', scatter_dimension=0, tiled=True)]
  transfers between devices with their start and end apart: 8 -> 3, of which waited for: 7 -> 3; matrix products, arithmetic and copies ran while one was open for 16% -> 2% of each run, Pallas kernels for 0% -> 0%
where the time goes in v1:
time: 567 us; the launch traced here: 564 us
  waiting for transfers between devices  370 us (65%)
  Pallas kernels  136 us (24%)
  blocking collectives  24.4 us (4%)
  between operations  13.2 us (2%)
  other arithmetic  9.03 us (2%)
  local copies, waits for them, and re-layouts  6.38 us (1%)
    all_gather x1, waiting for transfers between devices, body(): gram = lax.all_gather(gram, 'protein', axis=0, tiled=True)  274 us
    pallas_call x1, Pallas kernels, whitened(): pl.pallas_call(factor_kernel, out_shape=jax.ShapeDtypeStruct((panels, var...  136 us
    psum x1, waiting for transfers between devices, body(): lax.psum((gram_part, protein_sums, dose_sums, dose_squares), 'sample')  79.5 us
    reduce_scatter x1, waiting for transfers between devices, body(): lax.psum_scatter(cross_part, 'sample', scatter_dimension=0, tiled=True)  17 us
    all_gather x1, blocking collectives, body(): centred = lax.all_gather(centred, 'protein', axis=1, tiled=True)  12.3 us
    psum x1, blocking collectives, body(): lax.psum((gram_part, protein_sums, dose_sums, dose_squares), 'sample')  12.1 us
  transfers between devices with their start and end apart: 3, of which 3 were waited for; matrix products, arithmetic and copies ran while one was open for 2% of the time, Pallas kernels for 0%

profile of v1, /device:TPU:25, one launch (start us, length us, event | category | flops | bytes accessed | tf_op | source)
XLA Modules:
  0.0 563.5 jit_solution(10772408562941174968)
XLA Ops:
  6.5 0.0 all-reduce.3.cloned.1.call-start
  6.5 0.0 copy-start
  6.5 2.5 convolution_bitcast_fusion.1
  9.1 0.0 copy-done
  9.1 0.7 convolution_bitcast_fusion
  9.9 2.2 pad_maximum_fusion
  12.1 0.0 copy-start.1
  12.1 0.0 all-reduce.3.cloned.1.call-update
  12.1 0.0 reduce-scatter.2.cloned.1.call-start
  12.2 1.0 copy-done.1
  13.1 1.5 convolution_bitcast_fusion.2
  14.6 0.0 reduce-scatter.2.cloned.1.call-update
  14.6 0.0 all-gather.2.cloned.1.call-start
  14.7 79.5 %all-reduce.3.cloned.1.call-done = f32[2,2048,256]{1,2,0:T(8,128)} async-done(((f32[2,2048,256]{1,2,0:T(8,128)}), f32[2,2048,256]{1,2,0:T(8,128)}) %all-reduce.3.cloned.1.call-update) | async-done | bytes 4194320 | tf_op jit(solution)/shard_map/psum | solution.py:223
  94.2 4.7 broadcast_multiply_fusion
  98.9 5.4 copy.6
  104.3 0.0 all-gather.2.cloned.1.call-update
  104.4 0.1 convert_reduce_fusion.1
  104.5 0.2 convert_reduce_fusion.2
  104.7 12.1 %all-reduce = (f32[512]{0:T(512)S(1)}, f32[512]{0:T(512)S(1)}, f32[512]{0:T(512)S(1)}) all-reduce(f32[512]{0:T(512)S(1)} %get-tuple-element.6, f32[512]{0:T(512)S(1)} %get-tuple-element.5, f32[512]{0:T(512)S(1)} %convert_reduce_fusion.1), channel_id=1, replica_groups=mesh['sample'=8,'protein'=4] {'sample'}, use_global_device_ids=true, to_apply=%region_7.0 | all-reduce | flops 1536 | bytes 12288 | tf_op jit(solution)/shard_map/psum | solution.py:223
  116.7 0.1 dynamic-slice_multiply_fusion
  116.8 17.0 %reduce-scatter.2.cloned.1.call-done = f32[64,512]{1,0:T(8,128)} async-done(((f32[512,512]{1,0:T(8,128)}), f32[64,512]{1,0:T(8,128)}) %reduce-scatter.2.cloned.1.call-update) | async-done | bytes 131088 | tf_op jit(solution)/shard_map/reduce_scatter | solution.py:226
  133.8 1.0 subtract_divide_fusion
  134.8 12.3 %all_gather.7.centred = f32[64,2048]{1,0:T(8,128)S(1)} all-gather(f32[64,512]{1,0:T(8,128)S(1)} %subtract_divide_fusion), channel_id=1, replica_groups=mesh['sample'=8,'protein'=4] {'protein'}, dimensions={1}, use_global_device_ids=true | all-gather | bytes 655360 | tf_op jit(solution)/shard_map/all_gather | solution.py:237
  147.1 273.6 %all-gather.2.cloned.1.call-done.gram = f32[8,2048,256]{2,1,0:T(8,128)} async-done(((f32[2,2048,256]{2,1,0:T(8,128)}), f32[8,2048,256]{2,1,0:T(8,128)}) %all-gather.2.cloned.1.call-update) | async-done | bytes 16777232 | tf_op jit(solution)/shard_map/all_gather | solution.py:236
  420.7 135.5 %shard_map.28 = f32[8,64,256]{2,1,0:T(8,128)S(1)} custom-call(f32[8,2048,256]{2,1,0:T(8,128)} %all-gather.2.cloned.1.call-done.gram, f32[64,2048]{1,0:T(8,128)S(1)} %all_gather.7.centred), custom_call_target="tpu_custom_call" | custom-call | tf_op jit(solution)/shard_map/pallas_call | solution.py:177
  556.3 0.7 pad_maximum_fusion.1
  (1 shorter events, 0.0 us)
Async XLA Ops:
  6.5 87.7 %all-reduce.3.cloned.1.call-start = ((), (), s32[]{:S(2)}) async-start(), calls=%async_computation.1 | async-start | bytes 8388608 | tf_op jit(solution)/shard_map/psum | solution.py:223
  6.5 2.6 copy-start
  12.1 1.0 copy-start.1
  12.1 121.7 %reduce-scatter.2.cloned.1.call-start = ((), (), s32[]{:S(2)}) async-start(), calls=%async_computation.3 | async-start | bytes 1179648 | tf_op jit(solution)/shard_map/reduce_scatter | solution.py:226
  14.6 406.1 %all-gather.2.cloned.1.call-start = ((), (), s32[]{:S(2)}) async-start(), calls=%async_computation.2 | async-start | bytes 20971520 | tf_op jit(solution)/shard_map/all_gather | solution.py:236
Sparse Core Ops, SparseCore 0:
  12.2 81.9 all-reduce.2
  97.7 36.0 reduce-scatter.1
  135.4 285.2 all-gather.1

commit v2 on v1

--- a/solution.py
+++ b/solution.py
@@ -100,17 +100,27 @@
 
 
 def factor_kernel(gram, centred, out, matrix, work, first, second, full, high, low, sem):
-    panels, proteins, _ = gram.shape
-    variants = centred.shape[0]
+    groups = gram.shape[0]
+    panels = 2 * groups
+    proteins = panels * WIDE
+    variants = centred.shape[1]
     total = proteins + variants
-    copies = [
-        pltpu.make_async_copy(gram.at[p], matrix.at[p, pl.ds(0, proteins), :], sem.at[p])
-        for p in range(panels)
-    ]
+    copies = []
+    for z in range(groups):
+        cut = (panels - z) * WIDE
+        for p, start, size in ((z, 0, cut), (panels - 1 - z, cut, (z + 1) * WIDE)):
+            copies.append(
+                pltpu.make_async_copy(
+                    gram.at[z, pl.ds(start, size), :],
+                    matrix.at[p, pl.ds(p * WIDE, size), :],
+                    sem.at[p],
+                )
+            )
     for copy in copies:
         copy.start()
-    for p in range(panels):
-        matrix[p, proteins:, :] = centred[:, p * WIDE : (p + 1) * WIDE]
+    for z in range(groups):
+        matrix[z, proteins:, :] = centred[z, :, :WIDE]
+        matrix[panels - 1 - z, proteins:, :] = centred[z, :, WIDE:]
     for copy in copies:
         copy.wait()
     eye = (
@@ -171,9 +181,9 @@
 
 
 def whitened(gram, centred):
-    panels, proteins, _ = gram.shape
-    variants = centred.shape[0]
-    total = proteins + variants
+    panels = 2 * gram.shape[0]
+    variants = centred.shape[1]
+    total = panels * WIDE + variants
     return pl.pallas_call(
         factor_kernel,
         out_shape=jax.ShapeDtypeStruct((panels, variants, WIDE), jnp.float32),
@@ -196,48 +206,298 @@
     )(gram, centred)
 
 
+def dot_tn(left, right):
+    return lax.dot_general(
+        left, right, (((0,), (0,)), ((), ())), preferred_element_type=jnp.float32
+    )
+
+
+def gather_kernel(
+    chips,
+    groups,
+    proteins,
+    dosage,
+    full,
+    centred,
+    gram_part,
+    rest_part,
+    gram_pair,
+    rest_pair,
+    gram_in,
+    rest_in,
+    piece,
+    own_centred,
+    pair_send,
+    pair_recv,
+    chip_send,
+    chip_recv,
+    z_send,
+    z_recv,
+    plane_send,
+    plane_recv,
+    core_send,
+    core_recv,
+    local_sem,
+):
+    me = lax.axis_index("sample")
+    z = lax.axis_index("protein")
+    chip, core = me // 2, me % 2
+    partner = (chip * 2 + 1 - core, z)
+    samples = proteins.shape[0]
+    count = samples * 2 * chips
+    variants = dosage.shape[1] // (2 * chips)
+    rows = full.shape[1] // (2 * chips)
+    panels = 2 * groups
+    rest_rows = rest_part.shape[2]
+
+    def chip_at(d):
+        return (((chip + d) % chips) * 2 + core, z)
+
+    def z_at(d):
+        return (me, (z + d) % groups)
+
+    barrier = pltpu.get_barrier_semaphore()
+    peers = [partner]
+    peers += [chip_at(d) for d in range(1, chips)]
+    peers += [z_at(d) for d in range(1, groups)]
+    for peer in peers:
+        pl.semaphore_signal(barrier, inc=1, device_id=peer, device_id_type=pl.DeviceIdType.MESH)
+
+    def gram_block(i, carry):
+        later = (i + z) // panels
+        row = pl.multiple_of((z + i - later * (z + 1)) * WIDE, WIDE)
+        column = pl.multiple_of((z + later * (panels - 1 - 2 * z)) * WIDE, WIDE)
+        gram_part[pl.ds(pl.multiple_of(i * WIDE, WIDE), WIDE), :] = dot_tn(
+            proteins[:, pl.ds(row, WIDE)], proteins[:, pl.ds(column, WIDE)]
+        )
+        return carry
+
+    lax.fori_loop(0, panels + 1, gram_block, 0)
+    first = proteins[:, pl.ds(pl.multiple_of(z * WIDE, WIDE), WIDE)]
+    last = proteins[:, pl.ds(pl.multiple_of((panels - 1 - z) * WIDE, WIDE), WIDE)]
+    ones = jnp.ones((samples, HALF), jnp.bfloat16)
+    doses = dosage[...]
+    tables = (
+        dot_tn(doses, first),
+        dot_tn(doses, last),
+        jnp.concatenate([dot_tn(doses, ones), dot_tn(doses * doses, ones)], 1),
+    )
+    sums = [
+        jnp.dot(
+            jnp.ones((8, samples), jnp.bfloat16), side, preferred_element_type=jnp.float32
+        )
+        for side in (first, last)
+    ]
+    for owner in range(2 * chips):
+        for t in range(3):
+            rest_part[owner % 2, owner // 2, t * variants : (t + 1) * variants, :] = tables[t][
+                owner * variants : (owner + 1) * variants
+            ]
+        for t in range(2):
+            at = 3 * variants + 8 * t
+            rest_part[owner % 2, owner // 2, at : at + 8, :] = sums[t]
+    pl.semaphore_wait(barrier, len(peers))
+
+    def remote(source, target, send, recv, device):
+        copy = pltpu.make_async_remote_copy(
+            src_ref=source,
+            dst_ref=target,
+            send_sem=send,
+            recv_sem=recv,
+            device_id=device,
+            device_id_type=pl.DeviceIdType.MESH,
+        )
+        copy.start()
+        return copy
+
+    def own_rows(owner_core, owner_chip):
+        return pl.ds(pl.multiple_of((owner_core * chips + owner_chip) * rows, 8), rows)
+
+    half_rows = chips * rows
+    pairs = [
+        remote(
+            gram_part.at[pl.ds(pl.multiple_of((1 - core) * half_rows, 8), half_rows), :],
+            gram_pair,
+            pair_send.at[0],
+            pair_recv.at[0],
+            partner,
+        ),
+        remote(rest_part.at[1 - core], rest_pair, pair_send.at[1], pair_recv.at[1], partner),
+    ]
+    for copy in pairs:
+        copy.wait()
+    sends = []
+    for d in list(range(1, chips)) + [0]:
+        to = (chip + d) % chips
+        mine = own_rows(core, to)
+        there = pl.ds(pl.multiple_of(to * rows, 8), rows)
+        gram_part[mine, :] = gram_part[mine, :] + gram_pair[there, :]
+        rest_part[core, to] = rest_part[core, to] + rest_pair[to]
+        if d > 0:
+            sends.append(
+                remote(
+                    gram_part.at[mine, :],
+                    gram_in.at[d - 1],
+                    chip_send.at[0, d - 1],
+                    chip_recv.at[0, d - 1],
+                    chip_at(d),
+                )
+            )
+            sends.append(
+                remote(
+                    rest_part.at[core, to],
+                    rest_in.at[d - 1],
+                    chip_send.at[1, d - 1],
+                    chip_recv.at[1, d - 1],
+                    chip_at(d),
+                )
+            )
+    for copy in sends:
+        copy.wait()
+    total = gram_part[own_rows(core, chip), :]
+    rest = rest_part[core, chip]
+    for d in range(chips - 1):
+        total = total + gram_in[d]
+        rest = rest + rest_in[d]
+    piece[...] = total / count
+    dose_sums = rest[2 * variants : 3 * variants, :HALF]
+    dose_squares = rest[2 * variants : 3 * variants, HALF:]
+    means = dose_sums / count
+    spread = jnp.sqrt(dose_squares / count - means * means + 1e-05) * math.sqrt(count)
+    means = jnp.concatenate([means, means], 1)
+    spread = jnp.concatenate([spread, spread], 1)
+    for t in range(2):
+        at = 3 * variants + 8 * t
+        cross = rest[t * variants : (t + 1) * variants]
+        own_centred[:, t * WIDE : (t + 1) * WIDE] = (
+            cross - means * rest[at : at + 1, :]
+        ) / spread
+
+    landing = own_rows(core, chip)
+    local = [
+        pltpu.make_async_copy(piece, full.at[z, landing, :], local_sem.at[0]),
+        pltpu.make_async_copy(own_centred, centred.at[z], local_sem.at[1]),
+    ]
+    for copy in local:
+        copy.start()
+    over_z = []
+    for d in range(1, groups):
+        over_z.append(
+            remote(
+                piece,
+                full.at[z, landing, :],
+                z_send.at[0, d - 1],
+                z_recv.at[0, d - 1],
+                z_at(d),
+            )
+        )
+        over_z.append(
+            remote(
+                own_centred, centred.at[z], z_send.at[1, d - 1], z_recv.at[1, d - 1], z_at(d)
+            )
+        )
+    plane = [[] for _ in range(groups)]
+    to_core = []
+    for j in range(groups):
+        group = (z - j + groups) % groups
+        if j > 0:
+            over_z[2 * j - 2].wait_recv()
+        held = piece if j == 0 else full.at[group, landing, :]
+        for d in range(1, chips):
+            plane[j].append(
+                remote(
+                    held,
+                    full.at[group, landing, :],
+                    plane_send.at[j, d - 1],
+                    plane_recv.at[j, d - 1],
+                    chip_at(d),
+                )
+            )
+        to_core.append(
+            remote(
+                held,
+                full.at[group, landing, :],
+                core_send.at[j, 0],
+                core_recv.at[j, 0],
+                partner,
+            )
+        )
+    for j in range(groups):
+        group = (z - j + groups) % groups
+        for d in range(1, chips):
+            plane[j][d - 1].wait_recv()
+            came = own_rows(core, (chip - d + chips) % chips)
+            to_core.append(
+                remote(
+                    full.at[group, came, :],
+                    full.at[group, came, :],
+                    core_send.at[j, d],
+                    core_recv.at[j, d],
+                    partner,
+                )
+            )
+    for copy in local:
+        copy.wait()
+    for d in range(1, groups):
+        over_z[2 * d - 1].wait_recv()
+    for copy in over_z:
+        copy.wait_send()
+    for j in range(groups):
+        for copy in plane[j]:
+            copy.wait_send()
+    for copy in to_core:
+        copy.wait()
+
+
+def gathered(proteins, dosage):
+    groups = lax.axis_size("protein")
+    chips = lax.axis_size("sample") // 2
+    variants = dosage.shape[1] // (2 * chips)
+    gram_rows = (2 * groups + 1) * WIDE
+    rows = gram_rows // (2 * chips)
+    rest_rows = 3 * variants + 16
+    dma = pltpu.SemaphoreType.DMA
+    f32 = jnp.float32
+    return pl.pallas_call(
+        lambda *refs: gather_kernel(chips, groups, *refs),
+        out_shape=(
+            jax.ShapeDtypeStruct((groups, gram_rows, WIDE), f32),
+            jax.ShapeDtypeStruct((groups, variants, 2 * WIDE), f32),
+        ),
+        in_specs=[pl.BlockSpec(memory_space=pltpu.VMEM)] * 2,
+        out_specs=(pl.BlockSpec(memory_space=pl.ANY), pl.BlockSpec(memory_space=pl.ANY)),
+        scratch_shapes=[
+            pltpu.VMEM((gram_rows, WIDE), f32),
+            pltpu.VMEM((2, chips, rest_rows, WIDE), f32),
+            pltpu.VMEM((gram_rows // 2, WIDE), f32),
+            pltpu.VMEM((chips, rest_rows, WIDE), f32),
+            pltpu.VMEM((chips - 1, rows, WIDE), f32),
+            pltpu.VMEM((chips - 1, rest_rows, WIDE), f32),
+            pltpu.VMEM((rows, WIDE), f32),
+            pltpu.VMEM((variants, 2 * WIDE), f32),
+            dma((2,)),
+            dma((2,)),
+            dma((2, chips - 1)),
+            dma((2, chips - 1)),
+            dma((2, groups - 1)),
+            dma((2, groups - 1)),
+            dma((groups, chips - 1)),
+            dma((groups, chips - 1)),
+            dma((groups, chips)),
+            dma((groups, chips)),
+            dma((2,)),
+        ],
+        compiler_params=pltpu.CompilerParams(
+            collective_id=0, has_side_effects=True, vmem_limit_bytes=48 * 1024 * 1024
+        ),
+    )(proteins, dosage)
+
+
 def body(proteins, dosage):
-    total_proteins = proteins.shape[1]
-    groups = lax.axis_size("protein")
-    block_width = total_proteins // groups
-    column = lax.axis_index("protein")
-    sample_count = proteins.shape[0] * lax.axis_size("sample")
-    variant_rows = dosage.shape[1] // lax.axis_size("sample")
-    contract = (((0,), (0,)), ((), ()))
-    own_proteins = lax.dynamic_slice_in_dim(proteins, column * block_width, block_width, 1)
-    gram_part = jnp.stack(
-        [
-            lax.dot_general(
-                proteins,
-                own_proteins[:, p * WIDE : (p + 1) * WIDE],
-                contract,
-                preferred_element_type=jnp.float32,
-            )
-            for p in range(block_width // WIDE)
-        ]
-    )
-    cross_part = lax.dot_general(dosage, own_proteins, contract, preferred_element_type=jnp.float32)
-    protein_sums = jnp.sum(own_proteins, axis=0, dtype=jnp.float32)
-    dose_sums = jnp.sum(dosage, axis=0, dtype=jnp.float32)
-    dose_squares = jnp.sum(dosage * dosage, axis=0, dtype=jnp.float32)
-    gram_total, protein_sums, dose_sums, dose_squares = lax.psum(
-        (gram_part, protein_sums, dose_sums, dose_squares), "sample"
-    )
-    cross = lax.psum_scatter(cross_part, "sample", scatter_dimension=0, tiled=True)
-    row_start = lax.axis_index("sample") * variant_rows
-    dose_sums = lax.dynamic_slice_in_dim(dose_sums, row_start, variant_rows, 0)
-    dose_squares = lax.dynamic_slice_in_dim(dose_squares, row_start, variant_rows, 0)
-    gram = gram_total / sample_count
-    means = dose_sums / sample_count
-    spread = jnp.sqrt(dose_squares / sample_count - means * means + 1e-05)
-    centred = (cross - means[:, None] * protein_sums[None, :]) / (
-        spread[:, None] * math.sqrt(sample_count)
-    )
-    gram = lax.all_gather(gram, "protein", axis=0, tiled=True)
-    centred = lax.all_gather(centred, "protein", axis=1, tiled=True)
+    own = proteins.shape[1] // lax.axis_size("protein") // WIDE
+    gram, centred = gathered(proteins, dosage)
     scores = whitened(gram, centred)
-    own = block_width // WIDE
-    scores = lax.dynamic_slice_in_dim(scores, column * own, own, 0)
+    scores = lax.dynamic_slice_in_dim(scores, lax.axis_index("protein") * own, own, 0)
     return jnp.concatenate([scores[p] for p in range(own)], 1)
 
 

time: 567 us -> 234 us (0.41)
  waiting for transfers between devices: 370 us -> 0 us
  Pallas kernels: 136 us -> 231 us
  blocking collectives: 24.4 us -> 0 us
  between operations: 13.2 us -> 0.03 us
  other arithmetic: 9.03 us -> 0.67 us
    all_gather x1 -> x0, waiting for transfers between devices: 274 us -> none  [body(): gram = lax.all_gather(gram, 'protein', axis=0, tiled=True)]
    pallas_call x0 -> x1, Pallas kernels: none -> 97.2 us  [gathered(): pl.pallas_call(lambda *refs: gather_kernel(chips, groups, *refs), out_sha...]
    psum x1 -> x0, waiting for transfers between devices: 79.5 us -> none  [body(): lax.psum((gram_part, protein_sums, dose_sums, dose_squares), 'sample')]
    reduce_scatter x1 -> x0, waiting for transfers between devices: 17 us -> none  [body(): lax.psum_scatter(cross_part, 'sample', scatter_dimension=0, tiled=True)]
    all_gather x1 -> x0, blocking collectives: 12.3 us -> none  [body(): centred = lax.all_gather(centred, 'protein', axis=1, tiled=True)]
    psum x1 -> x0, blocking collectives: 12.1 us -> none  [body(): lax.psum((gram_part, protein_sums, dose_sums, dose_squares), 'sample')]
    div x3 -> x0, other arithmetic: 5.83 us -> none  [the longest x1 4.75 us: body(): gram = gram_total / sample_count]
  transfers between devices with their start and end apart: 3 -> 0, of which waited for: 3 -> 0; matrix products, arithmetic and copies ran while one was open for 2% -> 0% of each run, Pallas kernels for 0% -> 0%
where the time goes in v2:
time: 234 us
  Pallas kernels  231 us (99%)
  local copies, waits for them, and re-layouts  2.65 us (1%)
    pallas_call x1, Pallas kernels, whitened(): pl.pallas_call(factor_kernel, out_shape=jax.ShapeDtypeStruct((panels, var...  133 us
    pallas_call x1, Pallas kernels, gathered(): pl.pallas_call(lambda *refs: gather_kernel(chips, groups, *refs), out_sha...  97.2 us

profile of v2, /device:TPU:25, one launch (start us, length us, event | category | flops | bytes accessed | tf_op | source)
XLA Modules:
  0.0 234.0 jit_solution(5384823962025973962)
XLA Ops:
  0.0 0.0 copy-start
  0.0 1.6 copy-done
  1.6 0.0 copy-start.1
  1.6 1.0 copy-done.1
  2.6 97.2 %shard_map.28 = (f32[4,2304,256]{2,1,0:T(8,128)}, f32[4,64,512]{2,1,0:T(8,128)S(1)}) custom-call(bf16[512,2048]{1,0:T(8,128)(2,1)S(1)} %copy-done, bf16[512,512]{1,0:T(8,128)(2,1)S(1)} %copy-done.1), custom_call_target="tpu_custom_call" | custom-call | tf_op jit(solution)/shard_map/pallas_call | solution.py:461
  99.9 133.4 %shard_map.29 = f32[8,64,256]{2,1,0:T(8,128)S(1)} custom-call(f32[4,2304,256]{2,1,0:T(8,128)} %get-tuple-element.7.gram, f32[4,64,512]{2,1,0:T(8,128)S(1)} %get-tuple-element.8.centred), custom_call_target="tpu_custom_call" | custom-call | tf_op jit(solution)/shard_map/pallas_call | solution.py:187
  233.3 0.7 pad_maximum_fusion
  (1 shorter events, 0.0 us)
Async XLA Ops:
  0.0 1.6 copy-start
  1.6 1.0 copy-start.1

commit v3 on v2

--- a/solution.py
+++ b/solution.py
@@ -10,7 +10,7 @@
 SUB = 8
 HALF = 128
 WIDE = 256
-CHUNK = 512
+CHUNK = 1024
 
 
 def split(value):
@@ -28,10 +28,9 @@
 def product_nt(left, right):
     left_high, left_low = left
     right_high, right_low = right
-    return (
-        dot_nt(left_high, right_high)
-        + dot_nt(left_low, right_high)
-        + dot_nt(left_high, right_low)
+    return dot_nt(
+        jnp.concatenate([left_high, left_low, left_high], 1),
+        jnp.concatenate([right_high, right_high, right_low], 1),
     )
 
 
@@ -65,13 +64,22 @@
         ]
         scale = [None] * SUB
         lower = [[None] * SUB for _ in range(SUB)]
-        for k in range(SUB):
-            scale[k] = lax.rsqrt(entry[k][k])
-            for i in range(k + 1, SUB):
+        for k in range(0, SUB, 2):
+            one, cross, two = entry[k][k], entry[k + 1][k], entry[k + 1][k + 1]
+            minor = lax.rsqrt(one * two - cross * cross)
+            scale[k] = lax.rsqrt(one)
+            scale[k + 1] = one * scale[k] * minor
+            lower[k + 1][k] = cross * scale[k]
+            for i in range(k + 2, SUB):
                 lower[i][k] = entry[i][k] * scale[k]
-            for i in range(k + 1, SUB):
-                for m in range(k + 1, i + 1):
-                    entry[i][m] = entry[i][m] - lower[i][k] * lower[m][k]
+                lower[i][k + 1] = (
+                    entry[i][k + 1] - lower[i][k] * lower[k + 1][k]
+                ) * scale[k + 1]
+            for i in range(k + 2, SUB):
+                for m in range(k + 2, i + 1):
+                    entry[i][m] = (
+                        entry[i][m] - lower[i][k] * lower[m][k] - lower[i][k + 1] * lower[m][k + 1]
+                    )
         solved = [None] * SUB
         wide = lambda value: jnp.concatenate([value, value], 1)
         for i in range(SUB):
@@ -373,6 +381,18 @@
             cross - means * rest[at : at + 1, :]
         ) / spread
 
+    near = 2 if chips == 4 else chips - 1
+
+    def chip_near(d):
+        if near == chips - 1:
+            return (chip + d) % chips
+        return chip + 1 - 2 * (chip % 2) if d == 1 else (chip + 2) % 4
+
+    def chip_from(d):
+        if near == chips - 1:
+            return (chip - d + chips) % chips
+        return chip_near(d)
+
     landing = own_rows(core, chip)
     local = [
         pltpu.make_async_copy(piece, full.at[z, landing, :], local_sem.at[0]),
@@ -403,14 +423,14 @@
         if j > 0:
             over_z[2 * j - 2].wait_recv()
         held = piece if j == 0 else full.at[group, landing, :]
-        for d in range(1, chips):
+        for d in range(1, near + 1):
             plane[j].append(
                 remote(
                     held,
                     full.at[group, landing, :],
                     plane_send.at[j, d - 1],
                     plane_recv.at[j, d - 1],
-                    chip_at(d),
+                    (chip_near(d) * 2 + core, z),
                 )
             )
         to_core.append(
@@ -424,15 +444,39 @@
         )
     for j in range(groups):
         group = (z - j + groups) % groups
-        for d in range(1, chips):
+        for d in range(1, near + 1):
             plane[j][d - 1].wait_recv()
-            came = own_rows(core, (chip - d + chips) % chips)
+            came = own_rows(core, chip_from(d))
+            if near < chips - 1 and d == 2 - j % 2:
+                plane[j].append(
+                    remote(
+                        full.at[group, came, :],
+                        full.at[group, came, :],
+                        plane_send.at[j, near],
+                        plane_recv.at[j, near],
+                        (chip_near(3 - d) * 2 + core, z),
+                    )
+                )
             to_core.append(
                 remote(
                     full.at[group, came, :],
                     full.at[group, came, :],
                     core_send.at[j, d],
                     core_recv.at[j, d],
+                    partner,
+                )
+            )
+    if near < chips - 1:
+        for j in range(groups):
+            group = (z - j + groups) % groups
+            plane[j][near].wait_recv()
+            came = own_rows(core, 3 - chip)
+            to_core.append(
+                remote(
+                    full.at[group, came, :],
+                    full.at[group, came, :],
+                    core_send.at[j, chips - 1],
+                    core_recv.at[j, chips - 1],
                     partner,
                 )
             )

time: 234 us -> 221 us (0.944)
  Pallas kernels: 231 us -> 218 us
    pallas_call x1, Pallas kernels: 133 us -> 121 us  [whitened(): pl.pallas_call(factor_kernel, out_shape=jax.ShapeDtypeStruct((panels, var...]
where the time goes in v3:
time: 221 us
  Pallas kernels  218 us (99%)
  local copies, waits for them, and re-layouts  2.65 us (1%)
    pallas_call x1, Pallas kernels, whitened(): pl.pallas_call(factor_kernel, out_shape=jax.ShapeDtypeStruct((panels, var...  121 us
    pallas_call x1, Pallas kernels, gathered(): pl.pallas_call(lambda *refs: gather_kernel(chips, groups, *refs), out_sha...  97.3 us

profile of v3, /device:TPU:25, one launch (start us, length us, event | category | flops | bytes accessed | tf_op | source)
XLA Modules:
  0.0 221.3 jit_solution(18364347482890064247)
XLA Ops:
  0.0 0.0 copy-start
  0.0 1.6 copy-done
  1.6 0.0 copy-start.1
  1.6 1.0 copy-done.1
  2.6 97.3 %shard_map.28 = (f32[4,2304,256]{2,1,0:T(8,128)}, f32[4,64,512]{2,1,0:T(8,128)S(1)}) custom-call(bf16[512,2048]{1,0:T(8,128)(2,1)S(1)} %copy-done, bf16[512,512]{1,0:T(8,128)(2,1)S(1)} %copy-done.1), custom_call_target="tpu_custom_call" | custom-call | tf_op jit(solution)/shard_map/pallas_call | solution.py:505
  99.9 120.6 %shard_map.29 = f32[8,64,256]{2,1,0:T(8,128)S(1)} custom-call(f32[4,2304,256]{2,1,0:T(8,128)} %get-tuple-element.7.gram, f32[4,64,512]{2,1,0:T(8,128)S(1)} %get-tuple-element.8.centred), custom_call_target="tpu_custom_call" | custom-call | tf_op jit(solution)/shard_map/pallas_call | solution.py:195
  220.6 0.7 pad_maximum_fusion
  (1 shorter events, 0.0 us)
Async XLA Ops:
  0.0 1.6 copy-start
  1.6 1.0 copy-start.1

commit v4 on v3

--- a/solution.py
+++ b/solution.py
@@ -37,16 +37,6 @@
 def exact_dot(left, right):
     return jnp.dot(
         left, right, precision=lax.Precision.HIGHEST, preferred_element_type=jnp.float32
-    )
-
-
-def exact_nt(left, right):
-    return lax.dot_general(
-        left,
-        right,
-        (((1,), (1,)), ((), ())),
-        precision=lax.Precision.HIGHEST,
-        preferred_element_type=jnp.float32,
     )
 
 
@@ -142,8 +132,8 @@
         work[:, :HALF] = matrix[k, pl.ds(top, HALF), :HALF]
         work[:, HALF:] = eye
         inverse_factor(work, first)
-        below = exact_nt(matrix[k, pl.ds(mid, HALF), :HALF], first[...])
-        work[:, :HALF] = matrix[k, pl.ds(mid, HALF), HALF:] - exact_nt(below, below)
+        below = product_nt(split(matrix[k, pl.ds(mid, HALF), :HALF]), split(first[...]))
+        work[:, :HALF] = matrix[k, pl.ds(mid, HALF), HALF:] - product_nt(split(below), split(below))
         work[:, HALF:] = eye
         inverse_factor(work, second)
         full[:HALF, :HALF] = first[...]

time: 221 us -> 219 us (level)
  Pallas kernels: 218 us -> 215 us
    pallas_call x1, Pallas kernels: 121 us -> 118 us  [whitened(): pl.pallas_call(factor_kernel, out_shape=jax.ShapeDtypeStruct((panels, var...]
where the time goes in v4:
time: 219 us
  Pallas kernels  215 us (98%)
  local copies, waits for them, and re-layouts  2.65 us (1%)
    pallas_call x1, Pallas kernels, whitened(): pl.pallas_call(factor_kernel, out_shape=jax.ShapeDtypeStruct((panels, var...  118 us
    pallas_call x1, Pallas kernels, gathered(): pl.pallas_call(lambda *refs: gather_kernel(chips, groups, *refs), out_sha...  97.3 us

profile of v4, /device:TPU:25, one launch (start us, length us, event | category | flops | bytes accessed | tf_op | source)
XLA Modules:
  0.0 218.6 jit_solution(17744285397024820813)
XLA Ops:
  0.0 0.0 copy-start
  0.0 1.6 copy-done
  1.6 0.0 copy-start.1
  1.6 1.0 copy-done.1
  2.6 97.3 %shard_map.28 = (f32[4,2304,256]{2,1,0:T(8,128)}, f32[4,64,512]{2,1,0:T(8,128)S(1)}) custom-call(bf16[512,2048]{1,0:T(8,128)(2,1)S(1)} %copy-done, bf16[512,512]{1,0:T(8,128)(2,1)S(1)} %copy-done.1), custom_call_target="tpu_custom_call" | custom-call | tf_op jit(solution)/shard_map/pallas_call | solution.py:495
  99.9 118.0 %shard_map.29 = f32[8,64,256]{2,1,0:T(8,128)S(1)} custom-call(f32[4,2304,256]{2,1,0:T(8,128)} %get-tuple-element.7.gram, f32[4,64,512]{2,1,0:T(8,128)S(1)} %get-tuple-element.8.centred), custom_call_target="tpu_custom_call" | custom-call | tf_op jit(solution)/shard_map/pallas_call | solution.py:185
  217.9 0.7 pad_maximum_fusion
  (1 shorter events, 0.0 us)
Async XLA Ops:
  0.0 1.6 copy-start
  1.6 1.0 copy-start.1
